TPU v7x, 128 devices: a whole 4x4x4 slice. The times are simulated.
128 devices in a mesh: ctx: 64 (over y, z, x), srv: 2 (over core).
Axes of the slice: x: 4, y: 4, z: 4, core: 2. Of those that a mesh axis runs over, the one named last changes fastest.
Arguments:
- tokens: bfloat16 [16384, 2048], P('ctx'), may hold values from -6 to 6
- norm_gain: float32 [2048], replicated, may hold values from 0.5 to 2
- q_gain: float32 [128], replicated, may hold values from 0.7 to 16
- k_gain: float32 [128], replicated, may hold values from 0.7 to 16
- w_query: bfloat16 [2048, 2048], P(None, 'srv'), may hold values from -0.125 to 0.125
- w_key: bfloat16 [2048, 256], replicated, may hold values from -0.125 to 0.125
- w_value: bfloat16 [2048, 256], replicated, may hold values from -0.125 to 0.125
- w_out: bfloat16 [2048, 2048], P('srv'), may hold values from -0.125 to 0.125
- doc_lengths: int32 [4], replicated, may hold values from 1 to 10240, 16384 in all
- stretch_offsets: int32 [64], P('ctx'), may hold values from 0 to 24288, as said below
Outputs:
- attn_out: bfloat16 [16384, 2048], P(('ctx', 'srv'))
Inputs may be any that keep to these rules, and one draw needn't show every extreme that they name: `doc_lengths`: the lengths sum to 16384; the longest is exactly 10240. `stretch_offsets`: offsets rise from block to block by 256 to 511; the first is below 256; the last is exactly (63) * 256 + 32 * 255.
All inputs are finite; a program needn't handle non-finite values.
Results may differ from a plain program's by a relative error of at most 0.013.
The roundings to bfloat16 on the way count: a program that leaves them out, or rounds other values in their place, can miss the bound.
Values may be sent and summed in bfloat16 or wider, within the bound.
A program may use at most 128 MiB of HBM per device.

v0:
```python
import math

import jax
import jax.numpy as jnp
import numpy as np
from jax import lax
from jax.experimental import pallas as pl
from jax.experimental.pallas import tpu as pltpu
from jax.sharding import PartitionSpec as P

rope_base = 1000000.0
norm_eps = 1e-06
masked_score = -1e30
HEAD = 128
ROWS = 256
BLOCKS = 64
REACH = 40
MESH = pl.DeviceIdType.MESH
F32 = jnp.float32
BF16 = jnp.bfloat16

hop_table = (
    (16, 48, 4, 12, 1, 3),
    (32, 49, 8, 28, 17, 19),
    (35, 56, 21, 44, 5, 7),
    (20, 51, 11, 31, 13, 34),
    (23, 40, 38, 61, 45, 15),
    (33, 53, 55, 29, 57, 30),
    (27, 59, 42, 26, 62, 18),
    (0, 52, 39, 25, 9, 54),
    (0, 36, 22, 24, 41, 10),
    (0, 37, 0, 60, 6, 47),
    (0, 63, 0, 0, 14, 43),
    (0, 0, 0, 0, 46, 58),
    (0, 0, 0, 0, 50, 0),
    (0, 0, 0, 0, 2, 0),
)

ways = ((1, 0, 0), (3, 0, 0), (0, 1, 0), (0, 3, 0), (0, 0, 1), (0, 0, 3))


def apart(index):
    return (index // 16, index // 4 % 4, index % 4)


def joined(a, b, sign=1):
    y, z, x = ((p + sign * q) % 4 for p, q in zip(a, b))
    return y * 16 + z * 4 + x


SLOTS = len(hop_table)
STRIDE = 4


def plan():
    hops = {d: (s, w) for s, row in enumerate(hop_table) for w, d in enumerate(row) if d}
    carried = {
        at: [0 <= c - joined(apart(c), apart(d), -1) <= REACH for c in range(BLOCKS)] for d, at in hops.items()
    }
    for d, (s, w) in sorted(hops.items(), key=lambda hop: -hop[1][0]):
        parent = joined(apart(d), ways[w], -1)
        if parent:
            for c in range(BLOCKS):
                if carried[s, w][joined(apart(c), ways[w])]:
                    carried[hops[parent]][c] = True
    return carried


carried_at = plan()


def looked_up(i):
    flat = [d for row in hop_table for d in row]
    words = [sum(d << 6 * k for k, d in enumerate(flat[at : at + 5])) for at in range(0, len(flat), 5)]
    word, group = jnp.int32(words[0]), i // 5
    for k in range(1, len(words)):
        word = jnp.where(group == k, jnp.int32(words[k]), word)
    return lax.shift_right_logical(word, 6 * lax.rem(i, 5)) & 63


def spans(row):
    out, start = [], None
    for c in range(BLOCKS + 1):
        inside = c < BLOCKS and row[c]
        if inside and start is None:
            start = c
        if not inside and start is not None:
            out.append((start, c - 1))
            start = None
    return out


def among(row, chip):
    found = None
    for first, last in spans(row):
        one = (chip >= first) & (chip <= last)
        found = one if found is None else found | one
    return chip < 0 if found is None else found


def sine_cosine(angle):
    turns = jnp.floor(angle * (2.0 / math.pi) + 0.5)
    rest = angle
    for part in quarter_parts:
        rest = rest - turns * part
    square = rest * rest
    s = rest + rest * square * (
        -1.6666666666e-1 + square * (8.3333331876e-3 + square * (-1.9841270114e-4 + square * 2.7557314e-6))
    )
    c = 1.0 + square * (
        -0.5 + square * (4.16666666e-2 + square * (-1.3888888e-3 + square * (2.4801587e-5 - square * 2.7557e-7)))
    )
    quarter = turns.astype(jnp.int32) & 3
    odd = (quarter & 1) == 1
    sine, cosine = jnp.where(odd, c, s), jnp.where(odd, s, c)
    sine = jnp.where(quarter >= 2, -sine, sine)
    cosine = jnp.where((quarter == 1) | (quarter == 2), -cosine, cosine)
    return sine, cosine


def split_quarter():
    parts, left = [], math.pi / 2
    for _ in range(3):
        exponent = math.floor(math.log2(left))
        unit = 2.0 ** (exponent - 7)
        part = math.floor(left / unit) * unit
        parts.append(part)
        left -= part
    return (*parts, left)


quarter_parts = split_quarter()
score_scale_2 = math.log2(math.e) * HEAD ** (-0.5)


def scaled_and_rotated(x, gain, sine, cosine):
    x = x * lax.rsqrt(jnp.mean(x * x, axis=0, keepdims=True) + norm_eps) * gain
    a, b = x[:64], x[64:]
    return jnp.concatenate([a * cosine - b * sine, b * cosine + a * sine], axis=0)


def column(row_vector):
    square = jnp.broadcast_to(row_vector, (HEAD, HEAD)).T
    return jnp.concatenate([square, square], axis=1)


def kernel(
    tokens, norm_gain, q_gain, k_gain, frequency, w_query, w_key, w_value, w_out, doc_lengths, offsets,
    out, x_buf, normed, wkv, wq, wo, kv, q_t, score, weight, state, top, attended, sent, received,
    load_sem, q_sem, send_sem, recv_sem, swap_sem,
):
    chip, server = lax.axis_index("ctx"), lax.axis_index("srv")
    cy, cz, cx = chip // 16, lax.rem(chip // 4, 4), lax.rem(chip, 4)

    def moved(step, sign=1):
        dy, dz, dx = step
        if sign < 0:
            dy, dz, dx = (4 - dy) % 4, (4 - dz) % 4, (4 - dx) % 4
        return lax.rem(cy + dy, 4) * 16 + lax.rem(cz + dz, 4) * 4 + lax.rem(cx + dx, 4)

    neighbours = [moved(w) for w in ways]
    barrier = pltpu.get_barrier_semaphore()
    for n in neighbours:
        pl.semaphore_signal(barrier, inc=1, device_id={"ctx": n}, device_id_type=MESH)
    pl.semaphore_signal(barrier, inc=1, device_id={"srv": 1 - server}, device_id_type=MESH)

    lanes = pl.ds(pl.multiple_of(server * HEAD, HEAD), HEAD)
    load_x = pltpu.make_async_copy(tokens, x_buf, load_sem.at[0])
    load_k = pltpu.make_async_copy(w_key.at[:, lanes], wkv.at[:, :HEAD], load_sem.at[1])
    load_v = pltpu.make_async_copy(w_value.at[:, lanes], wkv.at[:, HEAD:], load_sem.at[2])
    load_o = pltpu.make_async_copy(w_out, wo, load_sem.at[3])
    load_q = [
        pltpu.make_async_copy(w_query.at[:, i * 256 : (i + 1) * 256], wq.at[i], q_sem.at[i]) for i in range(4)
    ]
    for copy in (load_x, load_k, load_v, *load_q, load_o):
        copy.start()

    offset = offsets[0]
    token_lane = lax.broadcasted_iota(jnp.int32, (8, ROWS), 1)
    position = (token_lane + offset).astype(F32)[:1]
    sine, cosine = sine_cosine(
        jnp.concatenate([frequency[...], frequency[...]], axis=1) * jnp.broadcast_to(position, (64, ROWS))
    )
    lengths = [doc_lengths[i] for i in range(4)]
    ends = [lengths[0]]
    for i in range(1, 4):
        ends.append(ends[-1] + lengths[i])
    starts = [jnp.int32(0), *ends[:3]]
    feature = lax.broadcasted_iota(jnp.int32, (1, HEAD), 1)
    first_of = jnp.full((1, HEAD), 1 << 30, jnp.int32)
    end_of = jnp.full((1, HEAD), 1 << 30, jnp.int32)
    for i in range(4):
        first_of = jnp.where(feature == i, starts[i], first_of)
        end_of = jnp.where(feature == i, ends[i], end_of)
    feature_row = lax.broadcasted_iota(jnp.int32, (HEAD, ROWS), 0)
    token = lax.broadcasted_iota(jnp.int32, (HEAD, ROWS), 1) + chip * ROWS
    barred = jnp.zeros((HEAD, ROWS), F32)
    for i in range(4):
        outside = (token < starts[i]) | (token >= ends[i])
        barred = jnp.where((feature_row == i) & outside, masked_score, barred)
    barred = barred.astype(BF16)
    for h in range(8):
        q_t[HEAD:, h * ROWS : (h + 1) * ROWS] = barred

    load_x.wait()

    def norm_rows(i, carry):
        at = pl.ds(pl.multiple_of(i * 32, 32), 32)
        x = x_buf[at, :].astype(F32)
        x = x * lax.rsqrt(jnp.mean(x * x, axis=1, keepdims=True) + norm_eps) * norm_gain[...]
        normed[at, :] = x.astype(BF16)
        return carry

    lax.fori_loop(0, 8, norm_rows, 0)

    load_k.wait()
    load_v.wait()
    pair = jnp.dot(normed[...], wkv[...], preferred_element_type=F32)
    key = scaled_and_rotated(pair[:, :HEAD].T, column(k_gain[...]), sine, cosine).T.astype(BF16)
    value = pair[:, HEAD:].T.astype(BF16)
    kv[chip, :, :HEAD] = key
    kv[chip, :HEAD, HEAD:] = value[:, :HEAD]
    kv[chip, HEAD:, HEAD:] = value[:, HEAD:]

    def gathered(w, at):
        bits = jnp.int32(0)
        for t in range(SLOTS):
            if (t, w) in carried_at:
                bits += jnp.where(among(carried_at[t, w], at), 1 << t, 0)
        return bits

    takes = [gathered(w, chip) for w in range(6)]
    gives = [gathered(w, neighbours[w]) for w in range(6)]

    def set_in(bits, t):
        return lax.rem(lax.shift_right_logical(bits, t), 2) == 1

    def behind(y, z, x):
        return lax.rem(y + 4, 4) * 16 + lax.rem(z + 4, 4) * 4 + lax.rem(x + 4, 4)

    def hop(t, w, block):
        at = t * 6 + w
        return pltpu.make_async_remote_copy(
            src_ref=kv.at[block],
            dst_ref=kv.at[block],
            send_sem=send_sem.at[at],
            recv_sem=recv_sem.at[at],
            device_id={"ctx": neighbours[w]},
            device_id_type=MESH,
        )

    def hand_on(t):
        for w in range(6):

            @pl.when(set_in(gives[w], t))
            def _():
                d, (uy, uz, ux) = looked_up(t * 6 + w), ways[w]
                block = behind(cy - d // 16 + uy % 3 - uy // 3, cz - lax.rem(d // 4, 4) + uz % 3 - uz // 3, cx - lax.rem(d, 4) + ux % 3 - ux // 3)
                hop(t, w, block).start()

    def arrive(t):
        for w in range(6):

            @pl.when(set_in(takes[w], t))
            def _():
                d = looked_up(t * 6 + w)
                hop(t, w, behind(cy - d // 16, cz - lax.rem(d // 4, 4), cx - lax.rem(d, 4))).wait_recv()

    pl.semaphore_wait(barrier, 7)
    hand_on(0)

    q_column = column(q_gain[...])
    for i in range(4):
        load_q[i].wait()
        two = jnp.dot(normed[...], wq[i], preferred_element_type=F32)
        for u in range(2):
            h = 2 * i + u
            x = scaled_and_rotated(two[:, u * HEAD : (u + 1) * HEAD].T, q_column, sine, cosine)
            q_t[:HEAD, h * ROWS : (h + 1) * ROWS] = x.astype(BF16)

    ones = jnp.ones((16, ROWS), BF16)

    def attend(block, own):
        key_at = lax.broadcasted_iota(jnp.int32, (ROWS, HEAD), 0) + block * ROWS
        segment = jnp.where((key_at >= first_of) & (key_at < end_of), 1.0, 0.0).astype(BF16)
        keys = jnp.concatenate([kv[block, :, :HEAD], segment], axis=1)
        values = jnp.concatenate([kv[block, :HEAD, HEAD:], kv[block, HEAD:, HEAD:]], axis=1)
        values = jnp.concatenate([values, ones], axis=0)
        for h in range(8):
            at = slice(h * ROWS, (h + 1) * ROWS)
            s = jnp.dot(keys, q_t[:, at], preferred_element_type=F32)
            if own:
                later = lax.broadcasted_iota(jnp.int32, s.shape, 0) > lax.broadcasted_iota(jnp.int32, s.shape, 1)
                s = jnp.where(later, masked_score, s)
            score[:, at] = s
        for h in range(8):
            at = slice(h * ROWS, (h + 1) * ROWS)
            s = score[:, at]
            highest = jnp.max(s, axis=0, keepdims=True) * score_scale_2
            if not own:
                before = top[:, at]
                highest = jnp.maximum(before, highest)
                state[:, at] = state[:, at] * jnp.exp2(before - highest)[:1]
            else:
                highest = jnp.broadcast_to(highest, (8, ROWS))
            top[:, at] = highest
            weight[:, at] = jnp.exp2(s * score_scale_2 - highest[:1]).astype(BF16)
        for h in range(8):
            at = slice(h * ROWS, (h + 1) * ROWS)
            mixed = jnp.dot(values, weight[:, at], preferred_element_type=F32)
            if own:
                state[:, at] = mixed
            else:
                state[:, at] += mixed

    attend(chip, True)

    def compute(i, carry):
        d = looked_up(i)
        block = behind(cy - d // 16, cz - lax.rem(d // 4, 4), cx - lax.rem(d, 4))

        @pl.when((block < chip) & (block >= chip - REACH))
        def _():
            attend(block, False)

        return carry

    def slot(t, carry):
        arrive(t - 1)

        @pl.when(t < SLOTS)
        def _():
            hand_on(t)

        first = (t - 1) * STRIDE
        lax.fori_loop(first, jnp.where(t < SLOTS, first + STRIDE, SLOTS * 6), compute, 0)
        return carry

    lax.fori_loop(1, SLOTS + 1, slot, 0)

    load_o.wait()
    for h in range(8):
        at = slice(h * ROWS, (h + 1) * ROWS)
        x = state[:HEAD, at] * (1.0 / state[HEAD : HEAD + 1, at])
        attended[:, h * HEAD : (h + 1) * HEAD] = x.T.astype(BF16)
    theirs = pl.ds(pl.multiple_of((1 - server) * HEAD, HEAD), HEAD)
    mine = pl.ds(pl.multiple_of(server * HEAD, HEAD), HEAD)
    swaps = []
    for n in range(4):
        at = slice(n * 512, (n + 1) * 512)
        sent[n] = jnp.dot(attended[theirs, :], wo[:, at], preferred_element_type=F32).astype(BF16)
        swap = pltpu.make_async_remote_copy(
            src_ref=sent.at[n],
            dst_ref=received.at[n],
            send_sem=swap_sem.at[0, n],
            recv_sem=swap_sem.at[1, n],
            device_id={"srv": 1 - server},
            device_id_type=MESH,
        )
        swap.start()
        swaps.append(swap)
    for n in range(4):
        at = slice(n * 512, (n + 1) * 512)
        part = jnp.dot(attended[mine, :], wo[:, at], preferred_element_type=F32)
        swaps[n].wait_recv()
        out[:, at] = (part + received[n].astype(F32)).astype(BF16)
    for n in range(4):
        swaps[n].wait_send()

    def left(t, carry):
        for w in range(6):

            @pl.when(set_in(gives[w], t))
            def _():
                hop(t, w, chip).wait_send()

        return carry

    lax.fori_loop(0, SLOTS, left, 0)


def local(
    tokens, norm_gain, q_gain, k_gain, w_query, w_key, w_value, w_out, doc_lengths, stretch_offsets
):
    frequency = rope_base ** (-2.0 * jnp.arange(HEAD // 2, dtype=F32) / HEAD)
    frequency = jnp.broadcast_to(frequency[:, None], (HEAD // 2, HEAD))
    vmem = pl.BlockSpec(memory_space=pltpu.VMEM)
    smem = pl.BlockSpec(memory_space=pltpu.SMEM)
    hbm = pl.BlockSpec(memory_space=pl.ANY)
    dma = pltpu.SemaphoreType.DMA
    return pl.pallas_call(
        kernel,
        out_shape=jax.ShapeDtypeStruct((HEAD, 2048), BF16),
        in_specs=[hbm, vmem, vmem, vmem, vmem, hbm, hbm, hbm, hbm, smem, smem],
        out_specs=vmem,
        scratch_shapes=[
            pltpu.VMEM((ROWS, 2048), BF16),
            pltpu.VMEM((ROWS, 2048), BF16),
            pltpu.VMEM((2048, 256), BF16),
            pltpu.VMEM((4, 2048, 256), BF16),
            pltpu.VMEM((1024, 2048), BF16),
            pltpu.VMEM((BLOCKS, ROWS, 256), BF16),
            pltpu.VMEM((256, 2048), BF16),
            pltpu.VMEM((ROWS, 2048), F32),
            pltpu.VMEM((ROWS, 2048), BF16),
            pltpu.VMEM((HEAD + 16, 2048), F32),
            pltpu.VMEM((8, 2048), F32),
            pltpu.VMEM((ROWS, 1024), BF16),
            pltpu.VMEM((4, HEAD, 512), BF16),
            pltpu.VMEM((4, HEAD, 512), BF16),
            dma((4,)),
            dma((4,)),
            dma((SLOTS * 6,)),
            dma((SLOTS * 6,)),
            dma((2, 4)),
        ],
        compiler_params=pltpu.CompilerParams(
            collective_id=0, has_side_effects=True, vmem_limit_bytes=60 * 2**20
        ),
        name="attention_layer",
    )(
        tokens,
        norm_gain.reshape(1, -1),
        q_gain.reshape(1, -1),
        k_gain.reshape(1, -1),
        frequency,
        w_query,
        w_key,
        w_value,
        w_out,
        doc_lengths,
        stretch_offsets,
    )


def solution(mesh):
    return jax.shard_map(
        local,
        mesh=mesh,
        in_specs=(
            P("ctx", None),
            P(),
            P(),
            P(),
            P(None, "srv"),
            P(),
            P(),
            P("srv", None),
            P(),
            P("ctx"),
        ),
        out_specs=P(("ctx", "srv"), None),
        check_vma=False,
    )
```

profile of v0, /device:TPU:25, one launch (start us, length us, event | category | flops | bytes accessed | tf_op | source)
XLA Modules:
  0.0 88.3 jit_solution(9099852522316542022)
XLA Ops:
  0.7 0.7 broadcast_in_dim.2.frequency
  1.4 85.0 %attention_layer.1 = bf16[128,2048]{1,0:T(8,128)(2,1)} custom-call(bf16[256,2048]{1,0:T(8,128)(2,1)} %tokens.1, f32[1,2048]{1,0:T(1,128)} %bitcast.3, f32[1,128]{1,0:T(1,128)} %bitcast.4, f32[1,128]{1,0:T(1,128)} %bitcast.5, f32[64,128]{1,0:T(8,128)} %broadcast_in_dim.2.frequency, bf16[2048,1024]{1,0:T(8,128)(2,1)} %w_query.1, bf16[2048,256]{1,0:T(8,128)(2,1)} %w_key.1, ...), custom_call_target="tpu_custom_call" | custom-call | tf_op jit(solution)/shard_map/attention_layer/pallas_call | solution.py:391
  86.4 1.9 %copy.13 = bf16[128,2048]{1,0:T(8,128)(2,1)} copy(bf16[128,2048]{1,0:T(8,128)(2,1)} %attention_layer.1) | data formatting | bytes 1048576
  (1 shorter events, 0.0 us)
where the time goes:
time: 88.5 us; the launch traced here: 88.3 us
  Pallas kernels  85 us (96%)
  local copies, waits for them, and re-layouts  2.58 us (3%)
    pallas_call x1, Pallas kernels, local(): pl.pallas_call(kernel, out_shape=jax.ShapeDtypeStruct((HEAD, 2048), BF16)...  85 us
    unnamed x1, local copies, waits for them, and re-layouts  1.88 us

commit v1 on v0

--- a/solution.py
+++ b/solution.py
@@ -15,25 +15,24 @@
 ROWS = 256
 BLOCKS = 64
 REACH = 40
+WIDE = 2048
 MESH = pl.DeviceIdType.MESH
 F32 = jnp.float32
 BF16 = jnp.bfloat16
 
 hop_table = (
     (16, 48, 4, 12, 1, 3),
-    (32, 49, 8, 28, 17, 19),
-    (35, 56, 21, 44, 5, 7),
-    (20, 51, 11, 31, 13, 34),
-    (23, 40, 38, 61, 45, 15),
-    (33, 53, 55, 29, 57, 30),
-    (27, 59, 42, 26, 62, 18),
-    (0, 52, 39, 25, 9, 54),
-    (0, 36, 22, 24, 41, 10),
-    (0, 37, 0, 60, 6, 47),
-    (0, 63, 0, 0, 14, 43),
-    (0, 0, 0, 0, 46, 58),
-    (0, 0, 0, 0, 50, 0),
-    (0, 0, 0, 0, 2, 0),
+    (0, 0, 0, 0, 0, 0),
+    (17, 52, 8, 28, 5, 7),
+    (0, 32, 20, 60, 49, 19),
+    (21, 53, 11, 29, 6, 55),
+    (35, 36, 56, 31, 9, 2),
+    (27, 37, 59, 24, 18, 10),
+    (47, 57, 39, 25, 61, 34),
+    (23, 54, 41, 30, 22, 15),
+    (43, 50, 38, 46, 26, 0),
+    (45, 63, 58, 13, 62, 14),
+    (40, 51, 0, 44, 33, 42),
 )
 
 ways = ((1, 0, 0), (3, 0, 0), (0, 1, 0), (0, 3, 0), (0, 0, 1), (0, 0, 3))
@@ -49,7 +48,7 @@
 
 
 SLOTS = len(hop_table)
-STRIDE = 4
+LAG = 2
 
 
 def plan():
@@ -146,7 +145,7 @@
 
 def kernel(
     tokens, norm_gain, q_gain, k_gain, frequency, w_query, w_key, w_value, w_out, doc_lengths, offsets,
-    out, x_buf, normed, wkv, wq, wo, kv, q_t, score, weight, state, top, attended, sent, received,
+    out, x_buf, normed, wkv, wq, wo, kv, q_t, score, peak, weight, factor, state, top, attended, sent, received,
     load_sem, q_sem, send_sem, recv_sem, swap_sem,
 ):
     chip, server = lax.axis_index("ctx"), lax.axis_index("srv")
@@ -178,9 +177,7 @@
     offset = offsets[0]
     token_lane = lax.broadcasted_iota(jnp.int32, (8, ROWS), 1)
     position = (token_lane + offset).astype(F32)[:1]
-    sine, cosine = sine_cosine(
-        jnp.concatenate([frequency[...], frequency[...]], axis=1) * jnp.broadcast_to(position, (64, ROWS))
-    )
+    sine, cosine = sine_cosine(column(frequency[...])[:64] * jnp.broadcast_to(position, (64, ROWS)))
     lengths = [doc_lengths[i] for i in range(4)]
     ends = [lengths[0]]
     for i in range(1, 4):
@@ -239,35 +236,26 @@
         return lax.rem(y + 4, 4) * 16 + lax.rem(z + 4, 4) * 4 + lax.rem(x + 4, 4)
 
     def hop(t, w, block):
-        at = t * 6 + w
         return pltpu.make_async_remote_copy(
             src_ref=kv.at[block],
             dst_ref=kv.at[block],
-            send_sem=send_sem.at[at],
-            recv_sem=recv_sem.at[at],
+            send_sem=send_sem.at[t * 6 + w],
+            recv_sem=recv_sem.at[t * 6 + w],
             device_id={"ctx": neighbours[w]},
             device_id_type=MESH,
         )
 
-    def hand_on(t):
-        for w in range(6):
-
-            @pl.when(set_in(gives[w], t))
-            def _():
-                d, (uy, uz, ux) = looked_up(t * 6 + w), ways[w]
-                block = behind(cy - d // 16 + uy % 3 - uy // 3, cz - lax.rem(d // 4, 4) + uz % 3 - uz // 3, cx - lax.rem(d, 4) + ux % 3 - ux // 3)
-                hop(t, w, block).start()
-
-    def arrive(t):
-        for w in range(6):
-
-            @pl.when(set_in(takes[w], t))
-            def _():
-                d = looked_up(t * 6 + w)
-                hop(t, w, behind(cy - d // 16, cz - lax.rem(d // 4, 4), cx - lax.rem(d, 4))).wait_recv()
+    def block_at(d, way=(0, 0, 0)):
+        uy, uz, ux = (u - 4 * (u == 3) for u in way)
+        return behind(cy - d // 16 + uy, cz - lax.rem(d // 4, 4) + uz, cx - lax.rem(d, 4) + ux)
 
     pl.semaphore_wait(barrier, 7)
-    hand_on(0)
+    for w in range(6):
+
+        @pl.when(set_in(gives[w], 0))
+        def _():
+            hop(0, w, chip).start()
+
 
     q_column = column(q_gain[...])
     for i in range(4):
@@ -280,63 +268,82 @@
 
     ones = jnp.ones((16, ROWS), BF16)
 
-    def attend(block, own):
+    def scores(block, turn, own=False):
         key_at = lax.broadcasted_iota(jnp.int32, (ROWS, HEAD), 0) + block * ROWS
         segment = jnp.where((key_at >= first_of) & (key_at < end_of), 1.0, 0.0).astype(BF16)
         keys = jnp.concatenate([kv[block, :, :HEAD], segment], axis=1)
-        values = jnp.concatenate([kv[block, :HEAD, HEAD:], kv[block, HEAD:, HEAD:]], axis=1)
-        values = jnp.concatenate([values, ones], axis=0)
-        for h in range(8):
-            at = slice(h * ROWS, (h + 1) * ROWS)
+        step = ROWS if own else WIDE
+        for at in range(0, 2048, step):
+            at = slice(at, at + step)
             s = jnp.dot(keys, q_t[:, at], preferred_element_type=F32)
             if own:
                 later = lax.broadcasted_iota(jnp.int32, s.shape, 0) > lax.broadcasted_iota(jnp.int32, s.shape, 1)
                 s = jnp.where(later, masked_score, s)
-            score[:, at] = s
-        for h in range(8):
-            at = slice(h * ROWS, (h + 1) * ROWS)
-            s = score[:, at]
-            highest = jnp.max(s, axis=0, keepdims=True) * score_scale_2
-            if not own:
-                before = top[:, at]
-                highest = jnp.maximum(before, highest)
-                state[:, at] = state[:, at] * jnp.exp2(before - highest)[:1]
-            else:
-                highest = jnp.broadcast_to(highest, (8, ROWS))
+            score[turn, :, at] = s
+            peak[turn, :, at] = jnp.max(s.reshape(ROWS // 8, 8, step), axis=0)
+
+    def softmax(turn):
+        for at in range(0, 2048, WIDE):
+            at = slice(at, at + WIDE)
+            before = top[:, at]
+            highest = jnp.maximum(before, jnp.max(peak[turn, :, at], axis=0, keepdims=True) * score_scale_2)
             top[:, at] = highest
-            weight[:, at] = jnp.exp2(s * score_scale_2 - highest[:1]).astype(BF16)
-        for h in range(8):
-            at = slice(h * ROWS, (h + 1) * ROWS)
-            mixed = jnp.dot(values, weight[:, at], preferred_element_type=F32)
-            if own:
-                state[:, at] = mixed
-            else:
-                state[:, at] += mixed
-
-    attend(chip, True)
+            factor[turn, :, at] = jnp.exp2(before - highest)
+            weight[turn, :, at] = jnp.exp2(score[turn, :, at] * score_scale_2 - highest[:1]).astype(BF16)
+
+    def mix(block, turn):
+        values = jnp.concatenate([kv[block, :HEAD, HEAD:], kv[block, HEAD:, HEAD:]], axis=1)
+        values = jnp.concatenate([values, ones], axis=0)
+        for at in range(0, 2048, WIDE):
+            at = slice(at, at + WIDE)
+            mixed = jnp.dot(values, weight[turn, :, at], preferred_element_type=F32)
+            state[:, at] = state[:, at] * factor[turn, :1, at] + mixed
+
+    state[...] = jnp.zeros_like(state)
+    top[...] = jnp.full_like(top, masked_score)
+    weight[1] = jnp.zeros_like(weight[1])
+    factor[1] = jnp.ones_like(factor[1])
+    scores(chip, 0, True)
 
     def compute(i, carry):
-        d = looked_up(i)
-        block = behind(cy - d // 16, cz - lax.rem(d // 4, 4), cx - lax.rem(d, 4))
-
-        @pl.when((block < chip) & (block >= chip - REACH))
+        count, last, second = carry
+        block = block_at(looked_up(i))
+        wanted = (block < chip) & (block >= chip - REACH)
+        for turn in range(2):
+
+            @pl.when(wanted & (lax.rem(count, 2) != turn))
+            def _():
+                scores(block, turn)
+                softmax(1 - turn)
+                mix(second, turn)
+
+        return jnp.where(wanted, count + 1, count), jnp.where(wanted, block, last), jnp.where(wanted, last, second)
+
+    def slot(t, carry):
+        before = jnp.maximum(t - LAG, 0)
+        for w in range(6):
+
+            @pl.when(set_in(takes[w], before) & (t >= LAG))
+            def _():
+                hop(before, w, block_at(looked_up(before * 6 + w))).wait_recv()
+
+        for w in range(6):
+
+            @pl.when(set_in(gives[w], t))
+            def _():
+                hop(t, w, block_at(looked_up(t * 6 + w), ways[w])).start()
+
+        first = before * 6
+        return lax.fori_loop(first, jnp.where(t >= LAG, first + 6, first), compute, carry)
+
+    count, last, second = lax.fori_loop(1, SLOTS + LAG, slot, (jnp.int32(0), chip, chip))
+    for turn in range(2):
+
+        @pl.when(lax.rem(count, 2) == turn)
         def _():
-            attend(block, False)
-
-        return carry
-
-    def slot(t, carry):
-        arrive(t - 1)
-
-        @pl.when(t < SLOTS)
-        def _():
-            hand_on(t)
-
-        first = (t - 1) * STRIDE
-        lax.fori_loop(first, jnp.where(t < SLOTS, first + STRIDE, SLOTS * 6), compute, 0)
-        return carry
-
-    lax.fori_loop(1, SLOTS + 1, slot, 0)
+            softmax(turn)
+            mix(second, 1 - turn)
+            mix(last, turn)
 
     load_o.wait()
     for h in range(8):
@@ -382,8 +389,8 @@
 def local(
     tokens, norm_gain, q_gain, k_gain, w_query, w_key, w_value, w_out, doc_lengths, stretch_offsets
 ):
-    frequency = rope_base ** (-2.0 * jnp.arange(HEAD // 2, dtype=F32) / HEAD)
-    frequency = jnp.broadcast_to(frequency[:, None], (HEAD // 2, HEAD))
+    half = jnp.arange(HEAD // 2, dtype=F32)
+    frequency = rope_base ** (-2.0 * jnp.concatenate([half, half]) / HEAD)
     vmem = pl.BlockSpec(memory_space=pltpu.VMEM)
     smem = pl.BlockSpec(memory_space=pltpu.SMEM)
     hbm = pl.BlockSpec(memory_space=pl.ANY)
@@ -401,8 +408,10 @@
             pltpu.VMEM((1024, 2048), BF16),
             pltpu.VMEM((BLOCKS, ROWS, 256), BF16),
             pltpu.VMEM((256, 2048), BF16),
-            pltpu.VMEM((ROWS, 2048), F32),
-            pltpu.VMEM((ROWS, 2048), BF16),
+            pltpu.VMEM((2, ROWS, 2048), F32),
+            pltpu.VMEM((2, 8, 2048), F32),
+            pltpu.VMEM((2, ROWS, 2048), BF16),
+            pltpu.VMEM((2, 8, 2048), F32),
             pltpu.VMEM((HEAD + 16, 2048), F32),
             pltpu.VMEM((8, 2048), F32),
             pltpu.VMEM((ROWS, 1024), BF16),
@@ -423,7 +432,7 @@
         norm_gain.reshape(1, -1),
         q_gain.reshape(1, -1),
         k_gain.reshape(1, -1),
-        frequency,
+        frequency.reshape(1, -1),
         w_query,
         w_key,
         w_value,

time: 88.5 us -> 70.7 us (0.80)
  Pallas kernels: 85 us -> 67.3 us
    pallas_call x1, Pallas kernels: 85 us -> 67.3 us  [local(): pl.pallas_call(kernel, out_shape=jax.ShapeDtypeStruct((HEAD, 2048), BF16)...]
where the time goes in v1:
time: 70.7 us; the launch traced here: 70.5 us
  Pallas kernels  67.3 us (95%)
  local copies, waits for them, and re-layouts  1.89 us (3%)
    pallas_call x1, Pallas kernels, local(): pl.pallas_call(kernel, out_shape=jax.ShapeDtypeStruct((HEAD, 2048), BF16)...  67.3 us
    unnamed x1, local copies, waits for them, and re-layouts  1.88 us

profile of v1, /device:TPU:25, one launch (start us, length us, event | category | flops | bytes accessed | tf_op | source)
XLA Modules:
  0.0 70.5 jit_solution(17444014378911025051)
XLA Ops:
  0.7 0.6 fusion.frequency
  1.3 67.3 %attention_layer.1 = bf16[128,2048]{1,0:T(8,128)(2,1)} custom-call(bf16[256,2048]{1,0:T(8,128)(2,1)} %tokens.1, f32[1,2048]{1,0:T(1,128)} %bitcast.3, f32[1,128]{1,0:T(1,128)} %bitcast.4, f32[1,128]{1,0:T(1,128)} %bitcast.5, f32[1,128]{1,0:T(1,128)} %fusion.frequency, bf16[2048,1024]{1,0:T(8,128)(2,1)} %w_query.1, bf16[2048,256]{1,0:T(8,128)(2,1)} %w_key.1, ...), custom_call_target="tpu_custom_call" | custom-call | tf_op jit(solution)/shard_map/attention_layer/pallas_call | solution.py:398
  68.6 1.9 %copy.13 = bf16[128,2048]{1,0:T(8,128)(2,1)} copy(bf16[128,2048]{1,0:T(8,128)(2,1)} %attention_layer.1) | data formatting | bytes 1048576
  (1 shorter events, 0.0 us)

commit v2 on v1

--- a/solution.py
+++ b/solution.py
@@ -15,7 +15,7 @@
 ROWS = 256
 BLOCKS = 64
 REACH = 40
-WIDE = 2048
+WIDE = 512
 MESH = pl.DeviceIdType.MESH
 F32 = jnp.float32
 BF16 = jnp.bfloat16
@@ -268,42 +268,43 @@
 
     ones = jnp.ones((16, ROWS), BF16)
 
-    def scores(block, turn, own=False):
+    def keys_of(block):
         key_at = lax.broadcasted_iota(jnp.int32, (ROWS, HEAD), 0) + block * ROWS
         segment = jnp.where((key_at >= first_of) & (key_at < end_of), 1.0, 0.0).astype(BF16)
-        keys = jnp.concatenate([kv[block, :, :HEAD], segment], axis=1)
-        step = ROWS if own else WIDE
-        for at in range(0, 2048, step):
-            at = slice(at, at + step)
-            s = jnp.dot(keys, q_t[:, at], preferred_element_type=F32)
-            if own:
-                later = lax.broadcasted_iota(jnp.int32, s.shape, 0) > lax.broadcasted_iota(jnp.int32, s.shape, 1)
-                s = jnp.where(later, masked_score, s)
-            score[turn, :, at] = s
-            peak[turn, :, at] = jnp.max(s.reshape(ROWS // 8, 8, step), axis=0)
-
-    def softmax(turn):
-        for at in range(0, 2048, WIDE):
-            at = slice(at, at + WIDE)
-            before = top[:, at]
-            highest = jnp.maximum(before, jnp.max(peak[turn, :, at], axis=0, keepdims=True) * score_scale_2)
-            top[:, at] = highest
-            factor[turn, :, at] = jnp.exp2(before - highest)
-            weight[turn, :, at] = jnp.exp2(score[turn, :, at] * score_scale_2 - highest[:1]).astype(BF16)
-
-    def mix(block, turn):
+        return jnp.concatenate([kv[block, :, :HEAD], segment], axis=1)
+
+    def values_of(block):
         values = jnp.concatenate([kv[block, :HEAD, HEAD:], kv[block, HEAD:, HEAD:]], axis=1)
-        values = jnp.concatenate([values, ones], axis=0)
-        for at in range(0, 2048, WIDE):
-            at = slice(at, at + WIDE)
-            mixed = jnp.dot(values, weight[turn, :, at], preferred_element_type=F32)
-            state[:, at] = state[:, at] * factor[turn, :1, at] + mixed
+        return jnp.concatenate([values, ones], axis=0)
+
+    def scores(keys, turn, at, own=False):
+        s = jnp.dot(keys, q_t[:, at], preferred_element_type=F32)
+        if own:
+            later = lax.broadcasted_iota(jnp.int32, s.shape, 0) > lax.broadcasted_iota(jnp.int32, s.shape, 1)
+            s = jnp.where(later, masked_score, s)
+        score[turn, :, at] = s
+        peak[turn, :, at] = jnp.max(s.reshape(ROWS // 8, 8, -1), axis=0)
+
+    def softmax(turn, at):
+        before = top[:, at]
+        highest = jnp.maximum(before, jnp.max(peak[turn, :, at], axis=0, keepdims=True) * score_scale_2)
+        top[:, at] = highest
+        factor[turn, :, at] = jnp.exp2(before - highest)
+        weight[turn, :, at] = jnp.exp2(score[turn, :, at] * score_scale_2 - highest[:1]).astype(BF16)
+
+    def mix(values, turn, at):
+        mixed = jnp.dot(values, weight[turn, :, at], preferred_element_type=F32)
+        state[:, at] = state[:, at] * factor[turn, :1, at] + mixed
+
+    groups = [slice(at, at + WIDE) for at in range(0, 2048, WIDE)]
 
     state[...] = jnp.zeros_like(state)
     top[...] = jnp.full_like(top, masked_score)
     weight[1] = jnp.zeros_like(weight[1])
     factor[1] = jnp.ones_like(factor[1])
-    scores(chip, 0, True)
+    own_keys = keys_of(chip)
+    for h in range(8):
+        scores(own_keys, 0, slice(h * ROWS, (h + 1) * ROWS), True)
 
     def compute(i, carry):
         count, last, second = carry
@@ -313,9 +314,11 @@
 
             @pl.when(wanted & (lax.rem(count, 2) != turn))
             def _():
-                scores(block, turn)
-                softmax(1 - turn)
-                mix(second, turn)
+                keys, values = keys_of(block), values_of(second)
+                for at in groups:
+                    scores(keys, turn, at)
+                    softmax(1 - turn, at)
+                    mix(values, turn, at)
 
         return jnp.where(wanted, count + 1, count), jnp.where(wanted, block, last), jnp.where(wanted, last, second)
 
@@ -341,9 +344,11 @@
 
         @pl.when(lax.rem(count, 2) == turn)
         def _():
-            softmax(turn)
-            mix(second, 1 - turn)
-            mix(last, turn)
+            before, now = values_of(second), values_of(last)
+            for at in groups:
+                softmax(turn, at)
+                mix(before, 1 - turn, at)
+                mix(now, turn, at)
 
     load_o.wait()
     for h in range(8):

time: 70.7 us -> 63.5 us (0.90)
  Pallas kernels: 67.3 us -> 60.2 us
    pallas_call x1, Pallas kernels: 67.3 us -> 60.2 us  [local(): pl.pallas_call(kernel, out_shape=jax.ShapeDtypeStruct((HEAD, 2048), BF16)...]
where the time goes in v2:
time: 63.5 us; the launch traced here: 63.3 us
  Pallas kernels  60.2 us (95%)
  local copies, waits for them, and re-layouts  1.89 us (3%)
  between operations  0.67 us (1%)
    pallas_call x1, Pallas kernels, local(): pl.pallas_call(kernel, out_shape=jax.ShapeDtypeStruct((HEAD, 2048), BF16)...  60.2 us
    unnamed x1, local copies, waits for them, and re-layouts  1.88 us

profile of v2, /device:TPU:25, one launch (start us, length us, event | category | flops | bytes accessed | tf_op | source)
XLA Modules:
  0.0 63.3 jit_solution(461308477463981181)
XLA Ops:
  0.7 0.6 fusion.frequency
  1.3 60.2 %attention_layer.1 = bf16[128,2048]{1,0:T(8,128)(2,1)} custom-call(bf16[256,2048]{1,0:T(8,128)(2,1)} %tokens.1, f32[1,2048]{1,0:T(1,128)} %bitcast.3, f32[1,128]{1,0:T(1,128)} %bitcast.4, f32[1,128]{1,0:T(1,128)} %bitcast.5, f32[1,128]{1,0:T(1,128)} %fusion.frequency, bf16[2048,1024]{1,0:T(8,128)(2,1)} %w_query.1, bf16[2048,256]{1,0:T(8,128)(2,1)} %w_key.1, ...), custom_call_target="tpu_custom_call" | custom-call | tf_op jit(solution)/shard_map/attention_layer/pallas_call | solution.py:403
  61.4 1.9 %copy.13 = bf16[128,2048]{1,0:T(8,128)(2,1)} copy(bf16[128,2048]{1,0:T(8,128)(2,1)} %attention_layer.1) | data formatting | bytes 1048576
  (1 shorter events, 0.0 us)

commit v3 on v2

--- a/solution.py
+++ b/solution.py
@@ -23,16 +23,16 @@
 hop_table = (
     (16, 48, 4, 12, 1, 3),
     (0, 0, 0, 0, 0, 0),
-    (17, 52, 8, 28, 5, 7),
-    (0, 32, 20, 60, 49, 19),
-    (21, 53, 11, 29, 6, 55),
-    (35, 36, 56, 31, 9, 2),
-    (27, 37, 59, 24, 18, 10),
-    (47, 57, 39, 25, 61, 34),
-    (23, 54, 41, 30, 22, 15),
-    (43, 50, 38, 46, 26, 0),
-    (45, 63, 58, 13, 62, 14),
-    (40, 51, 0, 44, 33, 42),
+    (28, 52, 20, 13, 17, 7),
+    (0, 32, 5, 8, 2, 19),
+    (29, 60, 56, 24, 21, 31),
+    (33, 55, 9, 44, 14, 18),
+    (47, 49, 23, 27, 25, 6),
+    (37, 39, 22, 30, 53, 63),
+    (35, 40, 36, 15, 26, 46),
+    (45, 57, 41, 10, 54, 38),
+    (0, 51, 11, 42, 34, 43),
+    (0, 50, 58, 59, 61, 62),
 )
 
 ways = ((1, 0, 0), (3, 0, 0), (0, 1, 0), (0, 3, 0), (0, 0, 1), (0, 0, 3))
@@ -199,6 +199,16 @@
     for h in range(8):
         q_t[HEAD:, h * ROWS : (h + 1) * ROWS] = barred
 
+    def gathered(w, at):
+        bits = jnp.int32(0)
+        for t in range(SLOTS):
+            if (t, w) in carried_at:
+                bits += jnp.where(among(carried_at[t, w], at), 1 << t, 0)
+        return bits
+
+    takes = [gathered(w, chip) for w in range(6)]
+    gives = [gathered(w, neighbours[w]) for w in range(6)]
+
     load_x.wait()
 
     def norm_rows(i, carry):
@@ -218,16 +228,6 @@
     kv[chip, :, :HEAD] = key
     kv[chip, :HEAD, HEAD:] = value[:, :HEAD]
     kv[chip, HEAD:, HEAD:] = value[:, HEAD:]
-
-    def gathered(w, at):
-        bits = jnp.int32(0)
-        for t in range(SLOTS):
-            if (t, w) in carried_at:
-                bits += jnp.where(among(carried_at[t, w], at), 1 << t, 0)
-        return bits
-
-    takes = [gathered(w, chip) for w in range(6)]
-    gives = [gathered(w, neighbours[w]) for w in range(6)]
 
     def set_in(bits, t):
         return lax.rem(lax.shift_right_logical(bits, t), 2) == 1
@@ -375,7 +375,7 @@
         at = slice(n * 512, (n + 1) * 512)
         part = jnp.dot(attended[mine, :], wo[:, at], preferred_element_type=F32)
         swaps[n].wait_recv()
-        out[:, at] = (part + received[n].astype(F32)).astype(BF16)
+        out[:, at] = part + received[n].astype(F32)
     for n in range(4):
         swaps[n].wait_send()
 
@@ -400,9 +400,9 @@
     smem = pl.BlockSpec(memory_space=pltpu.SMEM)
     hbm = pl.BlockSpec(memory_space=pl.ANY)
     dma = pltpu.SemaphoreType.DMA
-    return pl.pallas_call(
+    summed = pl.pallas_call(
         kernel,
-        out_shape=jax.ShapeDtypeStruct((HEAD, 2048), BF16),
+        out_shape=jax.ShapeDtypeStruct((HEAD, 2048), F32),
         in_specs=[hbm, vmem, vmem, vmem, vmem, hbm, hbm, hbm, hbm, smem, smem],
         out_specs=vmem,
         scratch_shapes=[
@@ -445,6 +445,7 @@
         doc_lengths,
         stretch_offsets,
     )
+    return summed.astype(BF16)
 
 
 def solution(mesh):

time: 63.5 us -> 63.3 us (level)
  other arithmetic: 0.59 us -> 2.68 us
  local copies, waits for them, and re-layouts: 1.89 us -> 0.01 us
    convert_element_type x0 -> x1, other arithmetic: none -> 2.09 us  [local(): return summed.astype(BF16)]
    unnamed x1 -> x0, local copies, waits for them, and re-layouts: 1.88 us -> none
where the time goes in v3:
time: 63.3 us; the launch traced here: 63.1 us
  Pallas kernels  59.8 us (94%)
  other arithmetic  2.68 us (4%)
  between operations  0.67 us (1%)
    pallas_call x1, Pallas kernels, local(): pl.pallas_call(kernel, out_shape=jax.ShapeDtypeStruct((HEAD, 2048), F32),...  59.8 us
    convert_element_type x1, other arithmetic, local(): return summed.astype(BF16)  2.09 us

profile of v3, /device:TPU:25, one launch (start us, length us, event | category | flops | bytes accessed | tf_op | source)
XLA Modules:
  0.0 63.1 jit_solution(16858895536603646208)
XLA Ops:
  0.7 0.6 fusion.frequency
  1.3 59.8 %attention_layer.1 = f32[128,2048]{1,0:T(8,128)} custom-call(bf16[256,2048]{1,0:T(8,128)(2,1)} %tokens.1, f32[1,2048]{1,0:T(1,128)} %bitcast.3, f32[1,128]{1,0:T(1,128)} %bitcast.4, f32[1,128]{1,0:T(1,128)} %bitcast.5, f32[1,128]{1,0:T(1,128)} %fusion.frequency, bf16[2048,1024]{1,0:T(8,128)(2,1)} %w_query.1, bf16[2048,256]{1,0:T(8,128)(2,1)} %w_key.1, ...), custom_call_target="tpu_custom_call" | custom-call | tf_op jit(solution)/shard_map/attention_layer/pallas_call | solution.py:403
  61.1 2.1 %convert_element_type.3 = bf16[128,2048]{1,0:T(8,128)(2,1)} convert(f32[128,2048]{1,0:T(8,128)} %attention_layer.1) | non-fusion elementwise | flops 262144 | bytes 1572864 | tf_op jit(solution)/shard_map/convert_element_type | solution.py:448
  (1 shorter events, 0.0 us)

commit v4 on v3

--- a/solution.py
+++ b/solution.py
@@ -375,7 +375,7 @@
         at = slice(n * 512, (n + 1) * 512)
         part = jnp.dot(attended[mine, :], wo[:, at], preferred_element_type=F32)
         swaps[n].wait_recv()
-        out[:, at] = part + received[n].astype(F32)
+        out[:, at] = (part + received[n].astype(F32)).astype(BF16)
     for n in range(4):
         swaps[n].wait_send()
 
@@ -400,9 +400,9 @@
     smem = pl.BlockSpec(memory_space=pltpu.SMEM)
     hbm = pl.BlockSpec(memory_space=pl.ANY)
     dma = pltpu.SemaphoreType.DMA
-    summed = pl.pallas_call(
+    return pl.pallas_call(
         kernel,
-        out_shape=jax.ShapeDtypeStruct((HEAD, 2048), F32),
+        out_shape=jax.ShapeDtypeStruct((HEAD, 2048), BF16),
         in_specs=[hbm, vmem, vmem, vmem, vmem, hbm, hbm, hbm, hbm, smem, smem],
         out_specs=vmem,
         scratch_shapes=[
@@ -445,7 +445,6 @@
         doc_lengths,
         stretch_offsets,
     )
-    return summed.astype(BF16)
 
 
 def solution(mesh):

time: 63.3 us -> 63 us (level)
  other arithmetic: 2.68 us -> 0.59 us
  local copies, waits for them, and re-layouts: 0.01 us -> 1.89 us
    convert_element_type x1 -> x0, other arithmetic: 2.09 us -> none  [local(): return summed.astype(BF16)]
    unnamed x0 -> x1, local copies, waits for them, and re-layouts: none -> 1.88 us
where the time goes in v4:
time: 63 us; the launch traced here: 62.8 us
  Pallas kernels  59.6 us (95%)
  local copies, waits for them, and re-layouts  1.89 us (3%)
  between operations  0.67 us (1%)
    pallas_call x1, Pallas kernels, local(): pl.pallas_call(kernel, out_shape=jax.ShapeDtypeStruct((HEAD, 2048), BF16)...  59.6 us
    unnamed x1, local copies, waits for them, and re-layouts  1.88 us

profile of v4, /device:TPU:25, one launch (start us, length us, event | category | flops | bytes accessed | tf_op | source)
XLA Modules:
  0.0 62.8 jit_solution(17370302508288278151)
XLA Ops:
  0.7 0.6 fusion.frequency
  1.3 59.6 %attention_layer.1 = bf16[128,2048]{1,0:T(8,128)(2,1)} custom-call(bf16[256,2048]{1,0:T(8,128)(2,1)} %tokens.1, f32[1,2048]{1,0:T(1,128)} %bitcast.3, f32[1,128]{1,0:T(1,128)} %bitcast.4, f32[1,128]{1,0:T(1,128)} %bitcast.5, f32[1,128]{1,0:T(1,128)} %fusion.frequency, bf16[2048,1024]{1,0:T(8,128)(2,1)} %w_query.1, bf16[2048,256]{1,0:T(8,128)(2,1)} %w_key.1, ...), custom_call_target="tpu_custom_call" | custom-call | tf_op jit(solution)/shard_map/attention_layer/pallas_call | solution.py:403
  60.9 1.9 %copy.13 = bf16[128,2048]{1,0:T(8,128)(2,1)} copy(bf16[128,2048]{1,0:T(8,128)(2,1)} %attention_layer.1) | data formatting | bytes 1048576
  (1 shorter events, 0.0 us)
